TPU v7x, 32 devices: a whole 2x2x4 slice. The times are simulated.
32 devices in a mesh: rows: 16 (over z, y, core), cols: 2 (over x).
Axes of the slice: x: 2, y: 2, z: 4, core: 2. Of those that a mesh axis runs over, the one named last changes fastest.
Arguments:
- start: float32 [16, 32768], P('cols', 'rows'), may hold values from -18 to 18
- weights: bfloat16 [256, 8, 128, 128], P('rows'), may hold values from 0 to 2, as said below
- block_count: int32 [256], P('rows'), may hold values from 1 to 8
- col_ids: int32 [256, 8], P('rows'), may hold values from 0 to 23
- send_ids: int32 [64, 2], P('rows'), may hold values from 0 to 15
- mixing: float32 [2, 16, 16], replicated, may hold values from -0.3 to 1.3
Outputs:
- subspace: float32 [16, 32768], P('cols', 'rows')
Inputs may be any that keep to these rules, and one draw needn't show every extreme that they name: `weights`: about one entry in 32 is nonzero, all nonzero entries positive.
All inputs are finite; a program needn't handle non-finite values.
Results may differ from a plain program's by a relative error of at most 0.034.
Values may be sent and summed in bfloat16 or wider, within the bound.
A program may use at most 64 MiB of HBM per device.

v0:
```python
import jax
import jax.numpy as jnp
from jax import lax
from jax.sharding import PartitionSpec as P

K = 16
NB = 8
REACH = 2
DEGREE = 4
ITERS = 2


filter_center = 1.2
filter_half = 0.8


def passed_along(block, axis, distance):
    devices = range(lax.axis_size(axis))
    route = [(i - distance, i) for i in devices if i - distance in devices]
    return lax.ppermute(block, axis, route)


def fetch_remote(outgoing):
    distances = [
        position - REACH if position < REACH else position - REACH + 1
        for position in range(2 * REACH)
    ]
    arrivals = [
        passed_along(outgoing[position], "rows", distances[position])
        for position in range(2 * REACH)
    ]
    return jnp.stack(arrivals, 0)


def apply_laplacian(vectors, scale, weights_live, col_ids, send_ids):
    scaled = (scale * vectors).astype(jnp.bfloat16)
    outgoing = scaled[send_ids]
    received = fetch_remote(outgoing)
    buffer = jnp.concatenate([scaled, received.reshape(-1, scaled.shape[1], scaled.shape[2])], 0)
    gathered = buffer[col_ids]
    products = jnp.einsum(
        "tbic,tbkc->tki", weights_live, gathered, preferred_element_type=jnp.float32
    )
    return vectors - scale * (products + scaled.astype(jnp.float32))


def body(start, weights, block_count, col_ids, send_ids, mixing):
    tile_count = weights.shape[0]
    tile_width = weights.shape[2]
    col_width = start.shape[0]
    row_devices = lax.axis_size("rows")
    total_points = tile_count * tile_width * row_devices
    my_col = lax.axis_index("cols")
    live = jnp.arange(NB, dtype=jnp.int32)[None, :] < block_count[:, None]
    weights_live = jnp.where(live[:, :, None, None], weights, jnp.zeros((), jnp.bfloat16))
    degree = 1.0 + jnp.sum(weights_live, axis=(1, 3), dtype=jnp.float32)
    scale = lax.rsqrt(degree)[:, None, :]
    vectors = start.reshape(col_width, tile_count, tile_width).transpose(1, 0, 2)
    for iteration in range(ITERS):
        previous = vectors
        current = (
            apply_laplacian(previous, scale, weights_live, col_ids, send_ids)
            - filter_center * previous
        ) / filter_half
        for order in range(DEGREE - 1):
            following = (
                2.0
                * (
                    apply_laplacian(current, scale, weights_live, col_ids, send_ids)
                    - filter_center * current
                )
                / filter_half
                - previous
            )
            previous, current = (current, following)
        every_column = lax.all_gather(current, "cols", axis=1, tiled=True)
        partial_gram = jnp.einsum(
            "tki,tli->kl", every_column, every_column, precision=lax.Precision.HIGHEST
        )
        gram = lax.psum(partial_gram, "rows") / total_points
        lower = jnp.linalg.cholesky(gram)
        inverse = lax.linalg.triangular_solve(
            lower, jnp.eye(K, dtype=jnp.float32), left_side=True, lower=True
        )
        combined = jnp.dot(mixing[iteration], inverse, precision=lax.Precision.HIGHEST)
        own_rows = lax.dynamic_slice_in_dim(combined, my_col * col_width, col_width, 0)
        vectors = jnp.einsum("kl,tli->tki", own_rows, every_column, precision=lax.Precision.HIGHEST)
    return vectors.transpose(1, 0, 2).reshape(col_width, tile_count * tile_width)


def solution(mesh):
    in_specs = (
        P("cols", "rows"),
        P("rows", None, None, None),
        P("rows"),
        P("rows", None),
        P("rows", None),
        P(),
    )
    out_specs = P("cols", "rows")
    return jax.shard_map(body, mesh=mesh, in_specs=in_specs, out_specs=out_specs, check_vma=False)
```

profile of v0, /device:TPU:0, one launch (start us, length us, event | category | flops | bytes accessed | tf_op | source)
XLA Modules:
  0.0 240.4 jit_solution(8107738918635692105)
XLA Ops:
  0.0 0.7 compare_select_fusion.1
  0.9 0.7 iota_compare_fusion.4
  1.6 3.2 %convert_reduce_fusion = f32[16,128]{1,0:T(8,128)S(1)} fusion(bf16[16,8,128,128]{3,2,1,0:T(8,128)(2,1)} %param.10, pred[16,8]{1,0:T(8,128)(4,1)S(1)} %iota_compare_fusion.4), kind=kLoop, calls=%fused_computation.16 | loop fusion | flops 6289408 | bytes 4202624 | tf_op jit(solution)/shard_map/reduce_sum | solution.py:56
  5.5 1.3 collective-permute-start
  6.8 2.4 collective-permute-start.2
  9.2 1.3 collective-permute-start.1
  10.5 7.4 %collective-permute-start.3 = (bf16[2,8,128]{2,1,0:T(8,128)(2,1)S(1)}, bf16[2,8,128]{2,1,0:T(8,128)(2,1)S(1)}, u32[]{:S(2)}, u32[]{:S(2)}) collective-permute-start(bf16[2,8,128]{2,1,0:T(8,128)(2,1)S(1)} %get-tuple-element.38), channel_id=1, source_target_pairs={{0,4},{2,6},{4,8},{6,10},{8,12},{10,14},{12,16},{14,18},{16,20},{1... | collective-permute-start | bytes 12296 | tf_op jit(solution)/shard_map/ppermute | solution.py:20
  18.1 1.1 collective-permute-done.3
  19.2 0.7 gather_fusion.1
  19.9 3.4 %multiply_convert_fusion.6 = (bf16[16,8,128]{2,1,0:T(8,128)(2,1)S(1)}, f32[16,8,128]{2,1,0:T(8,128)S(1)}) fusion(f32[16,128]{1,0:T(8,128)S(1)} %get-tuple-element.39, bf16[16,8,8,128]{3,2,1,0:T(8,128)(2,1)S(1)} %bitcast.233, bf16[16,8,128,128]{3,2,1,0:T(8,128)(2,1)} %param.10, pred[16,8]{1,0:T(8,128)(4,1)S(1)} %iota_compare_fusion.4, ...), kind=kOutput, calls=%fused_computation.83 | convolution fusion | flops 35815424 | bytes 4636800 | tf_op jit(solution)/shard_map/tbic,tbkc->tki/dot_general | solution.py:41
  24.0 1.3 collective-permute-start.4
  25.3 2.3 collective-permute-start.6
  27.6 1.3 collective-permute-start.5
  28.9 8.3 %collective-permute-start.7 = (bf16[2,8,128]{2,1,0:T(8,128)(2,1)S(1)}, bf16[2,8,128]{2,1,0:T(8,128)(2,1)S(1)}, u32[]{:S(2)}, u32[]{:S(2)}) collective-permute-start(bf16[2,8,128]{2,1,0:T(8,128)(2,1)S(1)} %get-tuple-element.34), channel_id=1, source_target_pairs={{0,4},{2,6},{4,8},{6,10},{8,12},{10,14},{12,16},{14,18},{16,20},{1... | collective-permute-start | bytes 12296 | tf_op jit(solution)/shard_map/ppermute | solution.py:20
  37.2 1.3 collective-permute-done.7
  38.5 0.7 gather_fusion.3
  39.2 3.5 %multiply_convert_fusion.5 = (bf16[16,8,128]{2,1,0:T(8,128)(2,1)S(1)}, f32[16,8,128]{2,1,0:T(8,128)S(1)}) fusion(f32[16,128]{1,0:T(8,128)S(1)} %get-tuple-element.40, f32[8,2048]{1,0:T(8,128)S(1)} %copy-done, f32[16,8,128]{2,1,0:T(8,128)S(1)} %get-tuple-element.42, f32[16,128]{1,0:T(8,128)S(1)} %get-tuple-element.39, ...), kind=kOutput, calls=%fused_computation.82 | convolution fusion | flops 35864576 | bytes 4702336 | tf_op jit(solution)/shard_map/tbic,tbkc->tki/dot_general | solution.py:41
  43.3 1.3 collective-permute-start.8
  44.6 2.6 %collective-permute-start.10 = (bf16[2,8,128]{2,1,0:T(8,128)(2,1)S(1)}, bf16[2,8,128]{2,1,0:T(8,128)(2,1)S(1)}, u32[]{:S(2)}, u32[]{:S(2)}) collective-permute-start(bf16[2,8,128]{2,1,0:T(8,128)(2,1)S(1)} %get-tuple-element.28), channel_id=1, source_target_pairs={{0,2},{2,4},{4,6},{6,8},{8,10},{10,12},{12,14},{14,16},{16,18},{18... | collective-permute-start | bytes 12296 | tf_op jit(solution)/shard_map/ppermute | solution.py:20
  47.2 1.3 collective-permute-start.9
  48.5 8.3 %collective-permute-start.11 = (bf16[2,8,128]{2,1,0:T(8,128)(2,1)S(1)}, bf16[2,8,128]{2,1,0:T(8,128)(2,1)S(1)}, u32[]{:S(2)}, u32[]{:S(2)}) collective-permute-start(bf16[2,8,128]{2,1,0:T(8,128)(2,1)S(1)} %get-tuple-element.30), channel_id=1, source_target_pairs={{0,4},{2,6},{4,8},{6,10},{8,12},{10,14},{12,16},{14,18},{16,20},{1... | collective-permute-start | bytes 12296 | tf_op jit(solution)/shard_map/ppermute | solution.py:20
  56.8 1.3 collective-permute-done.11
  58.8 3.5 %multiply_convert_fusion.4 = (bf16[16,8,128]{2,1,0:T(8,128)(2,1)S(1)}, f32[16,8,128]{2,1,0:T(8,128)S(1)}) fusion(f32[16,128]{1,0:T(8,128)S(1)} %get-tuple-element.40, f32[16,8,128]{2,1,0:T(8,128)S(1)} %get-tuple-element.42, f32[16,8,128]{2,1,0:T(8,128)S(1)} %get-tuple-element.44, bf16[16,8,8,128]{3,2,1,0:T(8,128)(2,1)S(1)} %bitcast.231, ...), kind=kOutput, calls=%fused_computation.81 | convolution fusion | flops 35864576 | bytes 4694144 | tf_op jit(solution)/shard_map/tbic,tbkc->tki/dot_general | solution.py:41
  62.8 1.3 collective-permute-start.12
  64.1 2.6 %collective-permute-start.14 = (bf16[2,8,128]{2,1,0:T(8,128)(2,1)S(1)}, bf16[2,8,128]{2,1,0:T(8,128)(2,1)S(1)}, u32[]{:S(2)}, u32[]{:S(2)}) collective-permute-start(bf16[2,8,128]{2,1,0:T(8,128)(2,1)S(1)} %get-tuple-element.24), channel_id=1, source_target_pairs={{0,2},{2,4},{4,6},{6,8},{8,10},{10,12},{12,14},{14,16},{16,18},{18... | collective-permute-start | bytes 12296 | tf_op jit(solution)/shard_map/ppermute | solution.py:20
  66.7 1.3 collective-permute-start.13
  68.0 8.3 %collective-permute-start.15 = (bf16[2,8,128]{2,1,0:T(8,128)(2,1)S(1)}, bf16[2,8,128]{2,1,0:T(8,128)(2,1)S(1)}, u32[]{:S(2)}, u32[]{:S(2)}) collective-permute-start(bf16[2,8,128]{2,1,0:T(8,128)(2,1)S(1)} %get-tuple-element.26), channel_id=1, source_target_pairs={{0,4},{2,6},{4,8},{6,10},{8,12},{10,14},{12,16},{14,18},{16,20},{1... | collective-permute-start | bytes 12296 | tf_op jit(solution)/shard_map/ppermute | solution.py:20
  76.4 1.3 collective-permute-done.15
  78.3 3.5 %fusion.25 = f32[16,8,128]{2,1,0:T(8,128)S(1)} fusion(f32[16,8,128]{2,1,0:T(8,128)S(1)} %get-tuple-element.44, f32[16,8,128]{2,1,0:T(8,128)S(1)} %get-tuple-element.46, bf16[16,8,8,128]{3,2,1,0:T(8,128)(2,1)S(1)} %bitcast.235, bf16[16,8,128,128]{3,2,1,0:T(8,128)(2,1)} %param.10, pred[16,8]{1,0:T(8,128)(4,1)S(1)} %iota_compare_fusion.4, ...), kind=kOutput, calls=%fused_computation.53 | convolution fusion | flops 35815424 | bytes 4661376 | tf_op jit(solution)/shard_map/tbic,tbkc->tki/dot_general | solution.py:41
  81.8 5.4 %all_gather.6 = f32[16,16,128]{2,1,0:T(8,128)S(1)} all-gather(f32[16,8,128]{2,1,0:T(8,128)S(1)} %fusion.25), channel_id=1, replica_groups=mesh['rows'=16,'cols'=2] {'cols'}, dimensions={1}, use_global_device_ids=true | all-gather | bytes 196608 | tf_op jit(solution)/shard_map/all_gather | solution.py:76
  87.4 33.2 %psum.14 = f32[16,16]{0,1:T(8,128)S(1)} all-reduce(f32[16,16]{0,1:T(8,128)S(1)} %convolution_bitcast_fusion.11), channel_id=1, replica_groups=mesh['rows'=16,'cols'=2] {'rows'}, use_global_device_ids=true, to_apply=%region_1.2 | all-reduce | flops 256 | bytes 2048 | tf_op jit(solution)/shard_map/psum | solution.py:80
  120.7 1.5 cholesky.44
  123.5 1.2 custom-call.6
  125.9 1.3 collective-permute-start.16
  127.2 1.3 collective-permute-start.18
  128.5 1.3 collective-permute-start.17
  129.8 7.5 %collective-permute-start.19 = (bf16[2,8,128]{2,1,0:T(8,128)(2,1)S(1)}, bf16[2,8,128]{2,1,0:T(8,128)(2,1)S(1)}, u32[]{:S(2)}, u32[]{:S(2)}) collective-permute-start(bf16[2,8,128]{2,1,0:T(8,128)(2,1)S(1)} %get-tuple-element.22), channel_id=1, source_target_pairs={{0,4},{2,6},{4,8},{6,10},{8,12},{10,14},{12,16},{14,18},{16,20},{1... | collective-permute-start | bytes 12296 | tf_op jit(solution)/shard_map/ppermute | solution.py:20
  137.4 1.3 collective-permute-done.19
  138.7 0.7 gather_fusion.9
  139.4 3.4 %multiply_convert_fusion.2 = (bf16[16,8,128]{2,1,0:T(8,128)(2,1)S(1)}, f32[16,8,128]{2,1,0:T(8,128)S(1)}) fusion(f32[16,128]{1,0:T(8,128)S(1)} %get-tuple-element.39, f32[16,8,128]{2,1,0:T(8,128)S(1)} %get-tuple-element.48, bf16[16,8,8,128]{3,2,1,0:T(8,128)(2,1)S(1)} %bitcast.236, bf16[16,8,128,128]{3,2,1,0:T(8,128)(2,1)} %param.10, ...), kind=kOutput, calls=%fused_computation.79 | convolution fusion | flops 35815424 | bytes 4636800 | tf_op jit(solution)/shard_map/tbic,tbkc->tki/dot_general | solution.py:41
  143.4 1.3 collective-permute-start.20
  144.7 1.3 collective-permute-start.22
  146.0 1.3 collective-permute-start.21
  147.3 7.8 %collective-permute-start.23 = (bf16[2,8,128]{2,1,0:T(8,128)(2,1)S(1)}, bf16[2,8,128]{2,1,0:T(8,128)(2,1)S(1)}, u32[]{:S(2)}, u32[]{:S(2)}) collective-permute-start(bf16[2,8,128]{2,1,0:T(8,128)(2,1)S(1)} %get-tuple-element.18), channel_id=1, source_target_pairs={{0,4},{2,6},{4,8},{6,10},{8,12},{10,14},{12,16},{14,18},{16,20},{1... | collective-permute-start | bytes 12296 | tf_op jit(solution)/shard_map/ppermute | solution.py:20
  155.1 1.3 collective-permute-done.23
  157.1 3.5 %multiply_convert_fusion.1 = (bf16[16,8,128]{2,1,0:T(8,128)(2,1)S(1)}, f32[16,8,128]{2,1,0:T(8,128)S(1)}) fusion(f32[16,128]{1,0:T(8,128)S(1)} %get-tuple-element.40, f32[16,8,128]{2,1,0:T(8,128)S(1)} %get-tuple-element.48, f32[16,8,128]{2,1,0:T(8,128)S(1)} %get-tuple-element.50, f32[16,128]{1,0:T(8,128)S(1)} %get-tuple-element.39, ...), kind=kOutput, calls=%fused_computation.78 | convolution fusion | flops 35864576 | bytes 4702336 | tf_op jit(solution)/shard_map/tbic,tbkc->tki/dot_general | solution.py:41
  161.2 1.3 collective-permute-start.24
  162.5 2.3 collective-permute-start.26
  164.8 1.3 collective-permute-start.25
  166.1 8.3 %collective-permute-start.27 = (bf16[2,8,128]{2,1,0:T(8,128)(2,1)S(1)}, bf16[2,8,128]{2,1,0:T(8,128)(2,1)S(1)}, u32[]{:S(2)}, u32[]{:S(2)}) collective-permute-start(bf16[2,8,128]{2,1,0:T(8,128)(2,1)S(1)} %get-tuple-element.14), channel_id=1, source_target_pairs={{0,4},{2,6},{4,8},{6,10},{8,12},{10,14},{12,16},{14,18},{16,20},{1... | collective-permute-start | bytes 12296 | tf_op jit(solution)/shard_map/ppermute | solution.py:20
  174.4 1.3 collective-permute-done.27
  176.4 3.5 %multiply_convert_fusion = (bf16[16,8,128]{2,1,0:T(8,128)(2,1)S(1)}, f32[16,8,128]{2,1,0:T(8,128)S(1)}) fusion(f32[16,128]{1,0:T(8,128)S(1)} %get-tuple-element.40, f32[16,8,128]{2,1,0:T(8,128)S(1)} %get-tuple-element.50, f32[16,8,128]{2,1,0:T(8,128)S(1)} %get-tuple-element.52, bf16[16,8,8,128]{3,2,1,0:T(8,128)(2,1)S(1)} %bitcast.232, ...), kind=kOutput, calls=%fused_computation.77 | convolution fusion | flops 35864576 | bytes 4694144 | tf_op jit(solution)/shard_map/tbic,tbkc->tki/dot_general | solution.py:41
  180.5 1.3 collective-permute-start.28
  181.8 2.6 %collective-permute-start.30 = (bf16[2,8,128]{2,1,0:T(8,128)(2,1)S(1)}, bf16[2,8,128]{2,1,0:T(8,128)(2,1)S(1)}, u32[]{:S(2)}, u32[]{:S(2)}) collective-permute-start(bf16[2,8,128]{2,1,0:T(8,128)(2,1)S(1)} %get-tuple-element.8), channel_id=1, source_target_pairs={{0,2},{2,4},{4,6},{6,8},{8,10},{10,12},{12,14},{14,16},{16,18},{18... | collective-permute-start | bytes 12296 | tf_op jit(solution)/shard_map/ppermute | solution.py:20
  184.4 1.3 collective-permute-start.29
  185.7 8.3 %collective-permute-start.31 = (bf16[2,8,128]{2,1,0:T(8,128)(2,1)S(1)}, bf16[2,8,128]{2,1,0:T(8,128)(2,1)S(1)}, u32[]{:S(2)}, u32[]{:S(2)}) collective-permute-start(bf16[2,8,128]{2,1,0:T(8,128)(2,1)S(1)} %get-tuple-element.10), channel_id=1, source_target_pairs={{0,4},{2,6},{4,8},{6,10},{8,12},{10,14},{12,16},{14,18},{16,20},{1... | collective-permute-start | bytes 12296 | tf_op jit(solution)/shard_map/ppermute | solution.py:20
  194.0 1.3 collective-permute-done.31
  195.3 0.7 gather_fusion.15
  196.0 3.5 %fusion.43 = f32[16,8,128]{2,1,0:T(8,128)S(1)} fusion(f32[16,8,128]{2,1,0:T(8,128)S(1)} %get-tuple-element.52, f32[16,8,128]{2,1,0:T(8,128)S(1)} %get-tuple-element.54, bf16[16,8,8,128]{3,2,1,0:T(8,128)(2,1)S(1)} %bitcast.229, bf16[16,8,128,128]{3,2,1,0:T(8,128)(2,1)} %param.10, pred[16,8]{1,0:T(8,128)(4,1)S(1)} %iota_compare_fusion.4, ...), kind=kOutput, calls=%fused_computation.71 | convolution fusion | flops 35815424 | bytes 4661376 | tf_op jit(solution)/shard_map/tbic,tbkc->tki/dot_general | solution.py:41
  199.4 5.4 %all_gather.7 = f32[16,16,128]{2,1,0:T(8,128)S(1)} all-gather(f32[16,8,128]{2,1,0:T(8,128)S(1)} %fusion.43), channel_id=1, replica_groups=mesh['rows'=16,'cols'=2] {'cols'}, dimensions={1}, use_global_device_ids=true | all-gather | bytes 196608 | tf_op jit(solution)/shard_map/all_gather | solution.py:76
  205.1 30.0 %psum.15 = f32[16,16]{0,1:T(8,128)S(1)} all-reduce(f32[16,16]{0,1:T(8,128)S(1)} %convolution_bitcast_fusion.10), channel_id=1, replica_groups=mesh['rows'=16,'cols'=2] {'rows'}, use_global_device_ids=true, to_apply=%region_4.7 | all-reduce | flops 256 | bytes 2048 | tf_op jit(solution)/shard_map/psum | solution.py:80
  235.2 1.5 cholesky.55
  238.0 1.2 custom-call.7
  239.6 0.8 convolution_bitcast_fusion
  (94 shorter events, 12.2 us)
Async XLA Ops:
  0.0 4.9 %copy-start = (f32[8,2048]{1,0:T(8,128)S(1)}, f32[8,2048]{1,0:T(8,128)}, u32[]{:S(2)}) copy-start(f32[8,2048]{1,0:T(8,128)} %param.9) | copy-start | bytes 196612
  0.0 17.9 %copy-start.2 = (s32[16,8]{0,1:T(8,128)S(1)}, s32[16,8]{0,1:T(8,128)}, u32[]{:S(2)}) copy-start(s32[16,8]{0,1:T(8,128)} %param.12) | copy-start | bytes 1540
  5.5 12.6 %collective-permute-start = (bf16[2,8,128]{2,1,0:T(8,128)(2,1)S(1)}, bf16[2,8,128]{2,1,0:T(8,128)(2,1)S(1)}, u32[]{:S(2)}, u32[]{:S(2)}) collective-permute-start(bf16[2,8,128]{2,1,0:T(8,128)(2,1)S(1)} %get-tuple-element.35), channel_id=1, source_target_pairs={{4,0},{6,2},{8,4},{10,6},{12,8},{14,10},{16,12},{18,14},{20,16},{2... | collective-permute-start | bytes 12296 | tf_op jit(solution)/shard_map/ppermute | solution.py:20
  6.8 11.3 %collective-permute-start.2 = (bf16[2,8,128]{2,1,0:T(8,128)(2,1)S(1)}, bf16[2,8,128]{2,1,0:T(8,128)(2,1)S(1)}, u32[]{:S(2)}, u32[]{:S(2)}) collective-permute-start(bf16[2,8,128]{2,1,0:T(8,128)(2,1)S(1)} %get-tuple-element.36), channel_id=1, source_target_pairs={{0,2},{2,4},{4,6},{6,8},{8,10},{10,12},{12,14},{14,16},{16,18},{18... | collective-permute-start | bytes 12296 | tf_op jit(solution)/shard_map/ppermute | solution.py:20
  9.2 8.9 %collective-permute-start.1 = (bf16[2,8,128]{2,1,0:T(8,128)(2,1)S(1)}, bf16[2,8,128]{2,1,0:T(8,128)(2,1)S(1)}, u32[]{:S(2)}, u32[]{:S(2)}) collective-permute-start(bf16[2,8,128]{2,1,0:T(8,128)(2,1)S(1)} %get-tuple-element.37), channel_id=1, source_target_pairs={{2,0},{4,2},{6,4},{8,6},{10,8},{12,10},{14,12},{16,14},{18,16},{20... | collective-permute-start | bytes 12296 | tf_op jit(solution)/shard_map/ppermute | solution.py:20
  10.5 8.7 %collective-permute-start.3 = (bf16[2,8,128]{2,1,0:T(8,128)(2,1)S(1)}, bf16[2,8,128]{2,1,0:T(8,128)(2,1)S(1)}, u32[]{:S(2)}, u32[]{:S(2)}) collective-permute-start(bf16[2,8,128]{2,1,0:T(8,128)(2,1)S(1)} %get-tuple-element.38), channel_id=1, source_target_pairs={{0,4},{2,6},{4,8},{6,10},{8,12},{10,14},{12,16},{14,18},{16,20},{1... | collective-permute-start | bytes 12296 | tf_op jit(solution)/shard_map/ppermute | solution.py:20
  24.0 13.2 %collective-permute-start.4 = (bf16[2,8,128]{2,1,0:T(8,128)(2,1)S(1)}, bf16[2,8,128]{2,1,0:T(8,128)(2,1)S(1)}, u32[]{:S(2)}, u32[]{:S(2)}) collective-permute-start(bf16[2,8,128]{2,1,0:T(8,128)(2,1)S(1)} %get-tuple-element.31), channel_id=1, source_target_pairs={{4,0},{6,2},{8,4},{10,6},{12,8},{14,10},{16,12},{18,14},{20,16},{2... | collective-permute-start | bytes 12296 | tf_op jit(solution)/shard_map/ppermute | solution.py:20
  25.3 11.9 %collective-permute-start.6 = (bf16[2,8,128]{2,1,0:T(8,128)(2,1)S(1)}, bf16[2,8,128]{2,1,0:T(8,128)(2,1)S(1)}, u32[]{:S(2)}, u32[]{:S(2)}) collective-permute-start(bf16[2,8,128]{2,1,0:T(8,128)(2,1)S(1)} %get-tuple-element.32), channel_id=1, source_target_pairs={{0,2},{2,4},{4,6},{6,8},{8,10},{10,12},{12,14},{14,16},{16,18},{18... | collective-permute-start | bytes 12296 | tf_op jit(solution)/shard_map/ppermute | solution.py:20
  27.6 9.6 %collective-permute-start.5 = (bf16[2,8,128]{2,1,0:T(8,128)(2,1)S(1)}, bf16[2,8,128]{2,1,0:T(8,128)(2,1)S(1)}, u32[]{:S(2)}, u32[]{:S(2)}) collective-permute-start(bf16[2,8,128]{2,1,0:T(8,128)(2,1)S(1)} %get-tuple-element.33), channel_id=1, source_target_pairs={{2,0},{4,2},{6,4},{8,6},{10,8},{12,10},{14,12},{16,14},{18,16},{20... | collective-permute-start | bytes 12296 | tf_op jit(solution)/shard_map/ppermute | solution.py:20
  28.9 9.6 %collective-permute-start.7 = (bf16[2,8,128]{2,1,0:T(8,128)(2,1)S(1)}, bf16[2,8,128]{2,1,0:T(8,128)(2,1)S(1)}, u32[]{:S(2)}, u32[]{:S(2)}) collective-permute-start(bf16[2,8,128]{2,1,0:T(8,128)(2,1)S(1)} %get-tuple-element.34), channel_id=1, source_target_pairs={{0,4},{2,6},{4,8},{6,10},{8,12},{10,14},{12,16},{14,18},{16,20},{1... | collective-permute-start | bytes 12296 | tf_op jit(solution)/shard_map/ppermute | solution.py:20
  43.3 13.5 %collective-permute-start.8 = (bf16[2,8,128]{2,1,0:T(8,128)(2,1)S(1)}, bf16[2,8,128]{2,1,0:T(8,128)(2,1)S(1)}, u32[]{:S(2)}, u32[]{:S(2)}) collective-permute-start(bf16[2,8,128]{2,1,0:T(8,128)(2,1)S(1)} %get-tuple-element.27), channel_id=1, source_target_pairs={{4,0},{6,2},{8,4},{10,6},{12,8},{14,10},{16,12},{18,14},{20,16},{2... | collective-permute-start | bytes 12296 | tf_op jit(solution)/shard_map/ppermute | solution.py:20
  44.6 12.2 %collective-permute-start.10 = (bf16[2,8,128]{2,1,0:T(8,128)(2,1)S(1)}, bf16[2,8,128]{2,1,0:T(8,128)(2,1)S(1)}, u32[]{:S(2)}, u32[]{:S(2)}) collective-permute-start(bf16[2,8,128]{2,1,0:T(8,128)(2,1)S(1)} %get-tuple-element.28), channel_id=1, source_target_pairs={{0,2},{2,4},{4,6},{6,8},{8,10},{10,12},{12,14},{14,16},{16,18},{18... | collective-permute-start | bytes 12296 | tf_op jit(solution)/shard_map/ppermute | solution.py:20
  47.2 9.6 %collective-permute-start.9 = (bf16[2,8,128]{2,1,0:T(8,128)(2,1)S(1)}, bf16[2,8,128]{2,1,0:T(8,128)(2,1)S(1)}, u32[]{:S(2)}, u32[]{:S(2)}) collective-permute-start(bf16[2,8,128]{2,1,0:T(8,128)(2,1)S(1)} %get-tuple-element.29), channel_id=1, source_target_pairs={{2,0},{4,2},{6,4},{8,6},{10,8},{12,10},{14,12},{16,14},{18,16},{20... | collective-permute-start | bytes 12296 | tf_op jit(solution)/shard_map/ppermute | solution.py:20
  48.5 9.6 %collective-permute-start.11 = (bf16[2,8,128]{2,1,0:T(8,128)(2,1)S(1)}, bf16[2,8,128]{2,1,0:T(8,128)(2,1)S(1)}, u32[]{:S(2)}, u32[]{:S(2)}) collective-permute-start(bf16[2,8,128]{2,1,0:T(8,128)(2,1)S(1)} %get-tuple-element.30), channel_id=1, source_target_pairs={{0,4},{2,6},{4,8},{6,10},{8,12},{10,14},{12,16},{14,18},{16,20},{1... | collective-permute-start | bytes 12296 | tf_op jit(solution)/shard_map/ppermute | solution.py:20
  62.2 62.7 %copy-start.1 = (f32[2,16,16]{2,1,0:T(8,128)S(1)}, f32[2,16,16]{2,1,0:T(8,128)}, u32[]{:S(2)}) copy-start(f32[2,16,16]{2,1,0:T(8,128)} %param.14) | copy-start | bytes 6148
  62.8 13.5 %collective-permute-start.12 = (bf16[2,8,128]{2,1,0:T(8,128)(2,1)S(1)}, bf16[2,8,128]{2,1,0:T(8,128)(2,1)S(1)}, u32[]{:S(2)}, u32[]{:S(2)}) collective-permute-start(bf16[2,8,128]{2,1,0:T(8,128)(2,1)S(1)} %get-tuple-element.23), channel_id=1, source_target_pairs={{4,0},{6,2},{8,4},{10,6},{12,8},{14,10},{16,12},{18,14},{20,16},{2... | collective-permute-start | bytes 12296 | tf_op jit(solution)/shard_map/ppermute | solution.py:20
  64.1 12.2 %collective-permute-start.14 = (bf16[2,8,128]{2,1,0:T(8,128)(2,1)S(1)}, bf16[2,8,128]{2,1,0:T(8,128)(2,1)S(1)}, u32[]{:S(2)}, u32[]{:S(2)}) collective-permute-start(bf16[2,8,128]{2,1,0:T(8,128)(2,1)S(1)} %get-tuple-element.24), channel_id=1, source_target_pairs={{0,2},{2,4},{4,6},{6,8},{8,10},{10,12},{12,14},{14,16},{16,18},{18... | collective-permute-start | bytes 12296 | tf_op jit(solution)/shard_map/ppermute | solution.py:20
  66.7 9.6 %collective-permute-start.13 = (bf16[2,8,128]{2,1,0:T(8,128)(2,1)S(1)}, bf16[2,8,128]{2,1,0:T(8,128)(2,1)S(1)}, u32[]{:S(2)}, u32[]{:S(2)}) collective-permute-start(bf16[2,8,128]{2,1,0:T(8,128)(2,1)S(1)} %get-tuple-element.25), channel_id=1, source_target_pairs={{2,0},{4,2},{6,4},{8,6},{10,8},{12,10},{14,12},{16,14},{18,16},{20... | collective-permute-start | bytes 12296 | tf_op jit(solution)/shard_map/ppermute | solution.py:20
  68.0 9.6 %collective-permute-start.15 = (bf16[2,8,128]{2,1,0:T(8,128)(2,1)S(1)}, bf16[2,8,128]{2,1,0:T(8,128)(2,1)S(1)}, u32[]{:S(2)}, u32[]{:S(2)}) collective-permute-start(bf16[2,8,128]{2,1,0:T(8,128)(2,1)S(1)} %get-tuple-element.26), channel_id=1, source_target_pairs={{0,4},{2,6},{4,8},{6,10},{8,12},{10,14},{12,16},{14,18},{16,20},{1... | collective-permute-start | bytes 12296 | tf_op jit(solution)/shard_map/ppermute | solution.py:20
  125.9 11.4 %collective-permute-start.16 = (bf16[2,8,128]{2,1,0:T(8,128)(2,1)S(1)}, bf16[2,8,128]{2,1,0:T(8,128)(2,1)S(1)}, u32[]{:S(2)}, u32[]{:S(2)}) collective-permute-start(bf16[2,8,128]{2,1,0:T(8,128)(2,1)S(1)} %get-tuple-element.19), channel_id=1, source_target_pairs={{4,0},{6,2},{8,4},{10,6},{12,8},{14,10},{16,12},{18,14},{20,16},{2... | collective-permute-start | bytes 12296 | tf_op jit(solution)/shard_map/ppermute | solution.py:20
  127.2 10.1 %collective-permute-start.18 = (bf16[2,8,128]{2,1,0:T(8,128)(2,1)S(1)}, bf16[2,8,128]{2,1,0:T(8,128)(2,1)S(1)}, u32[]{:S(2)}, u32[]{:S(2)}) collective-permute-start(bf16[2,8,128]{2,1,0:T(8,128)(2,1)S(1)} %get-tuple-element.20), channel_id=1, source_target_pairs={{0,2},{2,4},{4,6},{6,8},{8,10},{10,12},{12,14},{14,16},{16,18},{18... | collective-permute-start | bytes 12296 | tf_op jit(solution)/shard_map/ppermute | solution.py:20
  128.5 8.8 %collective-permute-start.17 = (bf16[2,8,128]{2,1,0:T(8,128)(2,1)S(1)}, bf16[2,8,128]{2,1,0:T(8,128)(2,1)S(1)}, u32[]{:S(2)}, u32[]{:S(2)}) collective-permute-start(bf16[2,8,128]{2,1,0:T(8,128)(2,1)S(1)} %get-tuple-element.21), channel_id=1, source_target_pairs={{2,0},{4,2},{6,4},{8,6},{10,8},{12,10},{14,12},{16,14},{18,16},{20... | collective-permute-start | bytes 12296 | tf_op jit(solution)/shard_map/ppermute | solution.py:20
  129.8 8.8 %collective-permute-start.19 = (bf16[2,8,128]{2,1,0:T(8,128)(2,1)S(1)}, bf16[2,8,128]{2,1,0:T(8,128)(2,1)S(1)}, u32[]{:S(2)}, u32[]{:S(2)}) collective-permute-start(bf16[2,8,128]{2,1,0:T(8,128)(2,1)S(1)} %get-tuple-element.22), channel_id=1, source_target_pairs={{0,4},{2,6},{4,8},{6,10},{8,12},{10,14},{12,16},{14,18},{16,20},{1... | collective-permute-start | bytes 12296 | tf_op jit(solution)/shard_map/ppermute | solution.py:20
  143.4 11.7 %collective-permute-start.20 = (bf16[2,8,128]{2,1,0:T(8,128)(2,1)S(1)}, bf16[2,8,128]{2,1,0:T(8,128)(2,1)S(1)}, u32[]{:S(2)}, u32[]{:S(2)}) collective-permute-start(bf16[2,8,128]{2,1,0:T(8,128)(2,1)S(1)} %get-tuple-element.15), channel_id=1, source_target_pairs={{4,0},{6,2},{8,4},{10,6},{12,8},{14,10},{16,12},{18,14},{20,16},{2... | collective-permute-start | bytes 12296 | tf_op jit(solution)/shard_map/ppermute | solution.py:20
  144.7 10.4 %collective-permute-start.22 = (bf16[2,8,128]{2,1,0:T(8,128)(2,1)S(1)}, bf16[2,8,128]{2,1,0:T(8,128)(2,1)S(1)}, u32[]{:S(2)}, u32[]{:S(2)}) collective-permute-start(bf16[2,8,128]{2,1,0:T(8,128)(2,1)S(1)} %get-tuple-element.16), channel_id=1, source_target_pairs={{0,2},{2,4},{4,6},{6,8},{8,10},{10,12},{12,14},{14,16},{16,18},{18... | collective-permute-start | bytes 12296 | tf_op jit(solution)/shard_map/ppermute | solution.py:20
  146.0 9.1 %collective-permute-start.21 = (bf16[2,8,128]{2,1,0:T(8,128)(2,1)S(1)}, bf16[2,8,128]{2,1,0:T(8,128)(2,1)S(1)}, u32[]{:S(2)}, u32[]{:S(2)}) collective-permute-start(bf16[2,8,128]{2,1,0:T(8,128)(2,1)S(1)} %get-tuple-element.17), channel_id=1, source_target_pairs={{2,0},{4,2},{6,4},{8,6},{10,8},{12,10},{14,12},{16,14},{18,16},{20... | collective-permute-start | bytes 12296 | tf_op jit(solution)/shard_map/ppermute | solution.py:20
  147.3 9.1 %collective-permute-start.23 = (bf16[2,8,128]{2,1,0:T(8,128)(2,1)S(1)}, bf16[2,8,128]{2,1,0:T(8,128)(2,1)S(1)}, u32[]{:S(2)}, u32[]{:S(2)}) collective-permute-start(bf16[2,8,128]{2,1,0:T(8,128)(2,1)S(1)} %get-tuple-element.18), channel_id=1, source_target_pairs={{0,4},{2,6},{4,8},{6,10},{8,12},{10,14},{12,16},{14,18},{16,20},{1... | collective-permute-start | bytes 12296 | tf_op jit(solution)/shard_map/ppermute | solution.py:20
  161.2 13.2 %collective-permute-start.24 = (bf16[2,8,128]{2,1,0:T(8,128)(2,1)S(1)}, bf16[2,8,128]{2,1,0:T(8,128)(2,1)S(1)}, u32[]{:S(2)}, u32[]{:S(2)}) collective-permute-start(bf16[2,8,128]{2,1,0:T(8,128)(2,1)S(1)} %get-tuple-element.11), channel_id=1, source_target_pairs={{4,0},{6,2},{8,4},{10,6},{12,8},{14,10},{16,12},{18,14},{20,16},{2... | collective-permute-start | bytes 12296 | tf_op jit(solution)/shard_map/ppermute | solution.py:20
  162.5 11.9 %collective-permute-start.26 = (bf16[2,8,128]{2,1,0:T(8,128)(2,1)S(1)}, bf16[2,8,128]{2,1,0:T(8,128)(2,1)S(1)}, u32[]{:S(2)}, u32[]{:S(2)}) collective-permute-start(bf16[2,8,128]{2,1,0:T(8,128)(2,1)S(1)} %get-tuple-element.12), channel_id=1, source_target_pairs={{0,2},{2,4},{4,6},{6,8},{8,10},{10,12},{12,14},{14,16},{16,18},{18... | collective-permute-start | bytes 12296 | tf_op jit(solution)/shard_map/ppermute | solution.py:20
  164.8 9.6 %collective-permute-start.25 = (bf16[2,8,128]{2,1,0:T(8,128)(2,1)S(1)}, bf16[2,8,128]{2,1,0:T(8,128)(2,1)S(1)}, u32[]{:S(2)}, u32[]{:S(2)}) collective-permute-start(bf16[2,8,128]{2,1,0:T(8,128)(2,1)S(1)} %get-tuple-element.13), channel_id=1, source_target_pairs={{2,0},{4,2},{6,4},{8,6},{10,8},{12,10},{14,12},{16,14},{18,16},{20... | collective-permute-start | bytes 12296 | tf_op jit(solution)/shard_map/ppermute | solution.py:20
  166.1 9.6 %collective-permute-start.27 = (bf16[2,8,128]{2,1,0:T(8,128)(2,1)S(1)}, bf16[2,8,128]{2,1,0:T(8,128)(2,1)S(1)}, u32[]{:S(2)}, u32[]{:S(2)}) collective-permute-start(bf16[2,8,128]{2,1,0:T(8,128)(2,1)S(1)} %get-tuple-element.14), channel_id=1, source_target_pairs={{0,4},{2,6},{4,8},{6,10},{8,12},{10,14},{12,16},{14,18},{16,20},{1... | collective-permute-start | bytes 12296 | tf_op jit(solution)/shard_map/ppermute | solution.py:20
  180.5 13.5 %collective-permute-start.28 = (bf16[2,8,128]{2,1,0:T(8,128)(2,1)S(1)}, bf16[2,8,128]{2,1,0:T(8,128)(2,1)S(1)}, u32[]{:S(2)}, u32[]{:S(2)}) collective-permute-start(bf16[2,8,128]{2,1,0:T(8,128)(2,1)S(1)} %get-tuple-element.6), channel_id=1, source_target_pairs={{4,0},{6,2},{8,4},{10,6},{12,8},{14,10},{16,12},{18,14},{20,16},{2... | collective-permute-start | bytes 12296 | tf_op jit(solution)/shard_map/ppermute | solution.py:20
  181.8 12.2 %collective-permute-start.30 = (bf16[2,8,128]{2,1,0:T(8,128)(2,1)S(1)}, bf16[2,8,128]{2,1,0:T(8,128)(2,1)S(1)}, u32[]{:S(2)}, u32[]{:S(2)}) collective-permute-start(bf16[2,8,128]{2,1,0:T(8,128)(2,1)S(1)} %get-tuple-element.8), channel_id=1, source_target_pairs={{0,2},{2,4},{4,6},{6,8},{8,10},{10,12},{12,14},{14,16},{16,18},{18... | collective-permute-start | bytes 12296 | tf_op jit(solution)/shard_map/ppermute | solution.py:20
  184.4 9.6 %collective-permute-start.29 = (bf16[2,8,128]{2,1,0:T(8,128)(2,1)S(1)}, bf16[2,8,128]{2,1,0:T(8,128)(2,1)S(1)}, u32[]{:S(2)}, u32[]{:S(2)}) collective-permute-start(bf16[2,8,128]{2,1,0:T(8,128)(2,1)S(1)} %get-tuple-element.9), channel_id=1, source_target_pairs={{2,0},{4,2},{6,4},{8,6},{10,8},{12,10},{14,12},{16,14},{18,16},{20... | collective-permute-start | bytes 12296 | tf_op jit(solution)/shard_map/ppermute | solution.py:20
  185.7 9.6 %collective-permute-start.31 = (bf16[2,8,128]{2,1,0:T(8,128)(2,1)S(1)}, bf16[2,8,128]{2,1,0:T(8,128)(2,1)S(1)}, u32[]{:S(2)}, u32[]{:S(2)}) collective-permute-start(bf16[2,8,128]{2,1,0:T(8,128)(2,1)S(1)} %get-tuple-element.10), channel_id=1, source_target_pairs={{0,4},{2,6},{4,8},{6,10},{8,12},{10,14},{12,16},{14,18},{16,20},{1... | collective-permute-start | bytes 12296 | tf_op jit(solution)/shard_map/ppermute | solution.py:20
where the time goes:
time: 242 us; the launch traced here: 240 us
  starting transfers between devices  102 us (42%)
  blocking collectives  74 us (31%)
  matrix products  29.8 us (12%)
  other arithmetic  12.9 us (5%)
  local copies, waits for them, and re-layouts  10.7 us (4%)
  waiting for transfers between devices  10.1 us (4%)
    ppermute x32, starting transfers between devices, passed_along(): return lax.ppermute(block, axis, route)  102 us
    psum x2, blocking collectives, body(): gram = lax.psum(partial_gram, 'rows') / total_points  63.3 us
    dot_general x8, matrix products, apply_laplacian(): jnp.einsum('tbic,tbkc->tki', weights_live, gathered, preferred_element_ty...  27.6 us
    all_gather x2, blocking collectives, body(): every_column = lax.all_gather(current, 'cols', axis=1, tiled=True)  10.8 us
    ppermute x32, waiting for transfers between devices, passed_along(): return lax.ppermute(block, axis, route)  10.1 us
    gather x8, local copies, waits for them, and re-layouts, apply_laplacian(): gathered = buffer[col_ids]  5.54 us
  transfers between devices with their start and end apart: 32, of which 8 were waited for; matrix products, arithmetic and copies ran while one was open for 0% of the time, Pallas kernels for 0%

commit v1 on v0

v1 whole, which is shorter than its diff:
```python
import functools

import jax
import jax.numpy as jnp
from jax import lax
from jax.experimental import pallas as pl
from jax.experimental.pallas import tpu as pltpu
from jax.sharding import PartitionSpec as P

K = 16
NB = 8
REACH = 2
SLOTS = 2
DEGREE = 4
ITERS = 2
SUB = 8
TILE = 128

filter_center = 1.2
filter_half = 0.8

MESH = pl.DeviceIdType.MESH
DISTANCES = [p - REACH if p < REACH else p - REACH + 1 for p in range(2 * REACH)]


def kernel(
    n, nx, group, col_width, tiles, total_points,
    block_count, col_ids, send_ids, start_ref, mixing_ref, weights_hbm,
    out_ref,
    w_ref, scale_ref, prev_ref, cur_ref, buf, outgoing, incoming, columns, gram_a, gram_b,
    w_sem, send_sem, recv_sem, col_send, col_recv, a_send, a_recv, b_send, b_recv,
):
    r = lax.axis_index("rows")
    x = lax.axis_index("cols")
    n_groups = n // group
    my_group, my_place = r // group, r % group

    barrier = pltpu.get_barrier_semaphore()
    greeted = (nx - 1) + (group - 1) + (n_groups - 1)
    for d in DISTANCES:
        reach = jnp.logical_and(r + d >= 0, r + d < n)

        @pl.when(reach)
        def _():
            pl.semaphore_signal(barrier, inc=1, device_id=(r + d, x), device_id_type=MESH)

        greeted = greeted + reach.astype(jnp.int32)
    for j in range(1, nx):
        pl.semaphore_signal(barrier, inc=1, device_id=(r, (x + j) % nx), device_id_type=MESH)
    for j in range(1, group):
        pl.semaphore_signal(
            barrier, inc=1, device_id=(my_group * group + (my_place + j) % group, x), device_id_type=MESH
        )
    for j in range(1, n_groups):
        pl.semaphore_signal(
            barrier, inc=1, device_id=((my_group + j) % n_groups * group + my_place, x), device_id_type=MESH
        )

    loads = [pltpu.make_async_copy(weights_hbm.at[t], w_ref.at[t], w_sem.at[t]) for t in range(tiles)]
    for load in loads:
        load.start()

    def times_tile(t, blocks):
        w = jnp.concatenate([w_ref[t, b] for b in range(NB)], 1)
        return lax.dot_general(
            blocks, w, (((1,), (1,)), ((), ())), preferred_element_type=jnp.float32
        )

    zeros = jnp.zeros((SUB, TILE), jnp.float32)
    for slot in range(tiles, tiles + 2 * REACH * SLOTS + 1):
        buf[slot] = zeros
    prev_ref[...] = start_ref[...]
    cur_ref[...] = start_ref[...]
    gram_a[...] = jnp.zeros_like(gram_a)
    for t in range(tiles):
        loads[t].wait()
        ones = [
            jnp.full((SUB, TILE), jnp.where(b < block_count[t], 1.0, 0.0), jnp.float32) for b in range(NB)
        ]
        degree = 1.0 + times_tile(t, jnp.concatenate(ones, 1).astype(jnp.bfloat16))
        scale_ref[:, t * TILE : (t + 1) * TILE] = lax.rsqrt(degree)

    pl.semaphore_wait(barrier, greeted)

    def neighbour_copy(step, o):
        return pltpu.make_async_remote_copy(
            src_ref=outgoing.at[step, o],
            dst_ref=incoming.at[step, o],
            send_sem=send_sem.at[step, o],
            recv_sem=recv_sem.at[step, o],
            device_id=(r + DISTANCES[o], x),
            device_id_type=MESH,
        )

    def apply(iteration, order):
        step = iteration * DEGREE + order
        for t in range(tiles):
            at = slice(t * TILE, (t + 1) * TILE)
            scaled = (scale_ref[:, at] * cur_ref[:, at]).astype(jnp.bfloat16)
            buf[t] = scaled.astype(jnp.float32)
        for o, d in enumerate(DISTANCES):
            picked = jnp.concatenate([buf[send_ids[o, s]] for s in range(SLOTS)], 0)
            outgoing[step, o] = picked.astype(jnp.bfloat16)

            @pl.when(jnp.logical_and(r + d >= 0, r + d < n))
            def _():
                neighbour_copy(step, o).start()

        for o, d in enumerate(DISTANCES):

            @pl.when(jnp.logical_and(r - d >= 0, r - d < n))
            def _():
                neighbour_copy(step, o).wait_recv()
                arrived = incoming[step, o].astype(jnp.float32)
                for s in range(SLOTS):
                    buf[tiles + o * SLOTS + s] = arrived[s * SUB : (s + 1) * SUB]

        first = order == 0
        gain = jnp.where(first, 1.0 / filter_half, 2.0 / filter_half)
        keep = jnp.where(first, 0.0, 1.0)
        empty = tiles + 2 * REACH * SLOTS
        for t in range(tiles):
            at = slice(t * TILE, (t + 1) * TILE)
            count = block_count[t]
            blocks = [buf[jnp.where(b < count, col_ids[t, b], empty)] for b in range(NB)]
            product = times_tile(t, jnp.concatenate(blocks, 1).astype(jnp.bfloat16))
            current = cur_ref[:, at]
            laplacian = current - scale_ref[:, at] * (product + buf[t])
            following = gain * (laplacian - filter_center * current) - keep * prev_ref[:, at]
            prev_ref[:, at] = current
            cur_ref[:, at] = following
        for o, d in enumerate(DISTANCES):

            @pl.when(jnp.logical_and(r + d >= 0, r + d < n))
            def _():
                neighbour_copy(step, o).wait_send()

    def exchange(copies):
        for copy in copies:
            copy.start()
        for copy in copies:
            copy.wait_recv()
        return copies

    def orthonormalize(iteration):
        columns[iteration, x] = cur_ref[...]
        mine = columns.at[iteration, x]
        pending = exchange([
            pltpu.make_async_remote_copy(
                src_ref=mine, dst_ref=mine,
                send_sem=col_send.at[iteration, j], recv_sem=col_recv.at[iteration, j],
                device_id=(r, (x + j) % nx), device_id_type=MESH,
            )
            for j in range(1, nx)
        ])
        every = jnp.concatenate([columns[iteration, j][:col_width] for j in range(nx)], 0)
        partial = lax.dot_general(
            every, every, (((1,), (1,)), ((), ())),
            precision=lax.Precision.HIGHEST, preferred_element_type=jnp.float32,
        )
        gram_a[iteration, my_place, :, 0:K] = partial
        mine_a = gram_a.at[iteration, my_place]
        pending += exchange([
            pltpu.make_async_remote_copy(
                src_ref=mine_a, dst_ref=mine_a,
                send_sem=a_send.at[iteration, j], recv_sem=a_recv.at[iteration, j],
                device_id=(my_group * group + (my_place + j) % group, x), device_id_type=MESH,
            )
            for j in range(1, group)
        ])
        gram_b[iteration, my_group] = sum(gram_a[iteration, j] for j in range(group))
        mine_b = gram_b.at[iteration, my_group]
        pending += exchange([
            pltpu.make_async_remote_copy(
                src_ref=mine_b, dst_ref=mine_b,
                send_sem=b_send.at[iteration, j], recv_sem=b_recv.at[iteration, j],
                device_id=((my_group + j) % n_groups * group + my_place, x), device_id_type=MESH,
            )
            for j in range(1, n_groups)
        ])
        gram = sum(gram_b[iteration, j] for j in range(n_groups)) / total_points
        row = lax.broadcasted_iota(jnp.int32, (K, TILE), 0)
        lane = lax.broadcasted_iota(jnp.int32, (K, TILE), 1)
        inverse = jnp.where(row == lane, 1.0, 0.0)
        for j in range(K - 1):
            factor = jnp.where(row > j, gram[:, j : j + 1] / gram[j : j + 1, j : j + 1], 0.0)
            inverse = inverse - factor * inverse[j : j + 1]
            gram = gram - factor * gram[j : j + 1]
        pivots = jnp.sum(jnp.where(row == lane, gram, 0.0), axis=1, keepdims=True)
        inverse = inverse * lax.rsqrt(pivots)
        combined = jnp.dot(
            mixing_ref[iteration, x], inverse,
            precision=lax.Precision.HIGHEST, preferred_element_type=jnp.float32,
        )
        vectors = jnp.dot(
            combined[:, :K], every,
            precision=lax.Precision.HIGHEST, preferred_element_type=jnp.float32,
        )
        prev_ref[...] = vectors
        cur_ref[...] = vectors
        for copy in pending:
            copy.wait_send()

    def one_iteration(iteration, carry):
        def one_order(order, inner):
            apply(iteration, order)
            return inner

        lax.fori_loop(0, DEGREE, one_order, 0)
        orthonormalize(iteration)
        return carry

    lax.fori_loop(0, ITERS, one_iteration, 0)
    out_ref[...] = cur_ref[...]


def body(start, weights, block_count, col_ids, send_ids, mixing):
    tiles = weights.shape[0]
    col_width, points = start.shape
    n, nx = lax.axis_size("rows"), lax.axis_size("cols")
    group = 4 if n % 4 == 0 else 1
    pad = SUB - col_width
    mixing = mixing.reshape(ITERS, nx, col_width, K)
    if pad:
        start = jnp.pad(start, ((0, pad), (0, 0)))
        mixing = jnp.pad(mixing, ((0, 0), (0, 0), (0, pad), (0, 0)))
    steps = ITERS * DEGREE
    vmem = pl.BlockSpec(memory_space=pltpu.VMEM)
    smem = pl.BlockSpec(memory_space=pltpu.SMEM)
    dma = pltpu.SemaphoreType.DMA
    out = pl.pallas_call(
        functools.partial(kernel, n, nx, group, col_width, tiles, float(points * n)),
        out_shape=jax.ShapeDtypeStruct((SUB, points), jnp.float32),
        in_specs=[smem, smem, smem, vmem, vmem, pl.BlockSpec(memory_space=pl.ANY)],
        out_specs=vmem,
        scratch_shapes=[
            pltpu.VMEM(weights.shape, jnp.bfloat16),
            pltpu.VMEM((SUB, points), jnp.float32),
            pltpu.VMEM((SUB, points), jnp.float32),
            pltpu.VMEM((SUB, points), jnp.float32),
            pltpu.VMEM((tiles + 2 * REACH * SLOTS + 1, SUB, TILE), jnp.float32),
            pltpu.VMEM((steps, 2 * REACH, SLOTS * SUB, TILE), jnp.bfloat16),
            pltpu.VMEM((steps, 2 * REACH, SLOTS * SUB, TILE), jnp.bfloat16),
            pltpu.VMEM((ITERS, nx, SUB, points), jnp.float32),
            pltpu.VMEM((ITERS, group, K, TILE), jnp.float32),
            pltpu.VMEM((ITERS, n // group, K, TILE), jnp.float32),
            dma((tiles,)),
            dma((steps, 2 * REACH)),
            dma((steps, 2 * REACH)),
            dma((ITERS, nx)),
            dma((ITERS, nx)),
            dma((ITERS, group)),
            dma((ITERS, group)),
            dma((ITERS, n // group)),
            dma((ITERS, n // group)),
        ],
        compiler_params=pltpu.CompilerParams(
            collective_id=0, has_side_effects=True, vmem_limit_bytes=32 * 1024 * 1024
        ),
    )(block_count, col_ids, send_ids, start, mixing, weights)
    return out[:col_width]


def solution(mesh):
    in_specs = (
        P("cols", "rows"),
        P("rows", None, None, None),
        P("rows"),
        P("rows", None),
        P("rows", None),
        P(),
    )
    out_specs = P("cols", "rows")
    return jax.shard_map(body, mesh=mesh, in_specs=in_specs, out_specs=out_specs, check_vma=False)
```

time: 242 us -> 72.8 us (0.30)
  starting transfers between devices: 102 us -> 0 us
  blocking collectives: 74 us -> 0 us
  Pallas kernels: 0 us -> 66 us
  matrix products: 29.8 us -> 0 us
  other arithmetic: 12.9 us -> 0 us
  waiting for transfers between devices: 10.1 us -> 0 us
  local copies, waits for them, and re-layouts: 10.7 us -> 6.55 us
    ppermute x32 -> x0, starting transfers between devices: 102 us -> none  [passed_along(): return lax.ppermute(block, axis, route)]
    pallas_call x0 -> x1, Pallas kernels: none -> 66 us  [body(): pl.pallas_call(functools.partial(kernel, n, nx, group, col_width, tiles,...]
    psum x2 -> x0, blocking collectives: 63.3 us -> none  [body(): gram = lax.psum(partial_gram, 'rows') / total_points]
    dot_general x14 -> x0, matrix products: 29.4 us -> none  [the longest x8 27.6 us: apply_laplacian(): jnp.einsum('tbic,tbkc->tki', weights_live, gathered, preferred_element_ty...]
    all_gather x2 -> x0, blocking collectives: 10.8 us -> none  [body(): every_column = lax.all_gather(current, 'cols', axis=1, tiled=True)]
    gather x16 -> x0, local copies, waits for them, and re-layouts: 10.2 us -> none  [the longest x8 5.54 us: apply_laplacian(): gathered = buffer[col_ids]]
    ppermute x32 -> x0, waiting for transfers between devices: 10.1 us -> none  [passed_along(): return lax.ppermute(block, axis, route)]
    another operation x18 -> x0, other arithmetic: 8.06 us -> none  [the longest x6 4.26 us: body(): lower = jnp.linalg.cholesky(gram)]
  transfers between devices with their start and end apart: 32 -> 0, of which waited for: 8 -> 0; matrix products, arithmetic and copies ran while one was open for 0% -> 0% of each run, Pallas kernels for 0% -> 0%
where the time goes in v1:
time: 72.8 us; the launch traced here: 72.5 us
  Pallas kernels  66 us (91%)
  local copies, waits for them, and re-layouts  6.55 us (9%)
    pallas_call x1, Pallas kernels, body(): pl.pallas_call(functools.partial(kernel, n, nx, group, col_width, tiles,...  66 us
    unnamed x11, local copies, waits for them, and re-layouts  6.55 us

profile of v1, /device:TPU:0, one launch (start us, length us, event | category | flops | bytes accessed | tf_op | source)
XLA Modules:
  0.0 72.5 jit_solution(14494038917215167444)
XLA Ops:
  0.0 0.8 %copy.8.send_ids = s32[4,2]{1,0:T(4,128)S(1)} copy(s32[4,2]{0,1:T(2,128)} %param.10) | data formatting | bytes 64 | tf_op args[4]
  0.8 0.8 %copy.7.col_ids = s32[16,8]{1,0:T(8,128)S(1)} copy(s32[16,8]{0,1:T(8,128)} %param.9) | data formatting | bytes 1024 | tf_op args[3]
  1.5 0.0 copy-start
  1.5 2.2 %copy-done = bf16[16,8,128,128]{3,2,1,0:T(8,128)(2,1)S(1)} copy-done((bf16[16,8,128,128]{3,2,1,0:T(8,128)(2,1)S(1)}, bf16[16,8,128,128]{3,2,1,0:T(8,128)(2,1)}, u32[]{:S(2)}) %copy-start) | copy-done | bytes 4194328
  3.7 0.0 copy-start.1
  3.7 0.8 %copy-done.1 = f32[8,2048]{1,0:T(8,128)S(1)} copy-done((f32[8,2048]{1,0:T(8,128)S(1)}, f32[8,2048]{1,0:T(8,128)}, u32[]{:S(2)}) %copy-start.1) | copy-done | bytes 65560
  4.6 0.0 copy-start.2
  4.6 0.7 copy-done.2
  5.3 0.0 copy-start.3
  5.3 0.7 copy-done.3
  5.9 66.0 %shard_map.64 = f32[8,2048]{1,0:T(8,128)S(1)} custom-call(s32[16]{0:T(128)S(1)} %copy-done.3, s32[16,8]{1,0:T(8,128)S(1)} %copy.7.col_ids, s32[4,2]{1,0:T(4,128)S(1)} %copy.8.send_ids, f32[8,2048]{1,0:T(8,128)S(1)} %copy-done.1, f32[2,2,8,16]{3,2,1,0:T(8,128)S(1)} %bitcast.1, bf16[16,8,128,128]{3,2,1,0:T(8,128)(2,1)S(1)} %copy-done), custom_call_target="tpu_custom_call" | custom-call | tf_op jit(solution)/shard_map/pallas_call | solution.py:231
  71.9 0.6 copy.10
Async XLA Ops:
  1.5 2.2 %copy-start = (bf16[16,8,128,128]{3,2,1,0:T(8,128)(2,1)S(1)}, bf16[16,8,128,128]{3,2,1,0:T(8,128)(2,1)}, u32[]{:S(2)}) copy-start(bf16[16,8,128,128]{3,2,1,0:T(8,128)(2,1)} %weights_hbm.1) | copy-start | bytes 12582916
  3.7 0.8 %copy-start.1 = (f32[8,2048]{1,0:T(8,128)S(1)}, f32[8,2048]{1,0:T(8,128)}, u32[]{:S(2)}) copy-start(f32[8,2048]{1,0:T(8,128)} %start_ref.1) | copy-start | bytes 196612
  4.6 0.7 copy-start.2
  5.3 0.7 copy-start.3

commit v2 on v1

--- a/solution.py
+++ b/solution.py
@@ -25,15 +25,29 @@
 
 def kernel(
     n, nx, group, col_width, tiles, total_points,
-    block_count, col_ids, send_ids, start_ref, mixing_ref, weights_hbm,
+    count_hbm, col_hbm, send_hbm, start_hbm, mixing_hbm, weights_hbm,
     out_ref,
+    block_count, col_ids, send_ids, mixing_ref,
     w_ref, scale_ref, prev_ref, cur_ref, buf, outgoing, incoming, columns, gram_a, gram_b,
-    w_sem, send_sem, recv_sem, col_send, col_recv, a_send, a_recv, b_send, b_recv,
+    w_sem, small_sem, send_sem, recv_sem, col_send, col_recv, a_send, a_recv, b_send, b_recv,
 ):
     r = lax.axis_index("rows")
     x = lax.axis_index("cols")
     n_groups = n // group
     my_group, my_place = r // group, r % group
+
+    smalls = [
+        pltpu.make_async_copy(src, dst, small_sem.at[i])
+        for i, (src, dst) in enumerate((
+            (count_hbm, block_count), (col_hbm, col_ids), (send_hbm, send_ids),
+            (mixing_hbm, mixing_ref), (start_hbm, columns.at[x]),
+        ))
+    ]
+    loads = [pltpu.make_async_copy(weights_hbm.at[t], w_ref.at[t], w_sem.at[t]) for t in range(tiles)]
+    for load in smalls + loads:
+        load.start()
+    buf[tiles:] = jnp.zeros((buf.shape[0] - tiles, K, TILE), jnp.bfloat16)
+    gram_a[...] = jnp.zeros_like(gram_a)
 
     barrier = pltpu.get_barrier_semaphore()
     greeted = (nx - 1) + (group - 1) + (n_groups - 1)
@@ -56,9 +70,16 @@
             barrier, inc=1, device_id=((my_group + j) % n_groups * group + my_place, x), device_id_type=MESH
         )
 
-    loads = [pltpu.make_async_copy(weights_hbm.at[t], w_ref.at[t], w_sem.at[t]) for t in range(tiles)]
-    for load in loads:
-        load.start()
+    pl.semaphore_wait(barrier, greeted)
+    column_copies = [
+        pltpu.make_async_remote_copy(
+            src_ref=start_hbm, dst_ref=columns.at[x], send_sem=col_send.at[j], recv_sem=col_recv.at[j],
+            device_id=(r, (x + j) % nx), device_id_type=MESH,
+        )
+        for j in range(1, nx)
+    ]
+    for copy in column_copies:
+        copy.start()
 
     def times_tile(t, blocks):
         w = jnp.concatenate([w_ref[t, b] for b in range(NB)], 1)
@@ -66,21 +87,20 @@
             blocks, w, (((1,), (1,)), ((), ())), preferred_element_type=jnp.float32
         )
 
-    zeros = jnp.zeros((SUB, TILE), jnp.float32)
-    for slot in range(tiles, tiles + 2 * REACH * SLOTS + 1):
-        buf[slot] = zeros
-    prev_ref[...] = start_ref[...]
-    cur_ref[...] = start_ref[...]
-    gram_a[...] = jnp.zeros_like(gram_a)
+    for small in smalls:
+        small.wait()
     for t in range(tiles):
         loads[t].wait()
         ones = [
-            jnp.full((SUB, TILE), jnp.where(b < block_count[t], 1.0, 0.0), jnp.float32) for b in range(NB)
+            jnp.full((K, TILE), jnp.where(b < block_count[t], 1.0, 0.0), jnp.float32) for b in range(NB)
         ]
         degree = 1.0 + times_tile(t, jnp.concatenate(ones, 1).astype(jnp.bfloat16))
         scale_ref[:, t * TILE : (t + 1) * TILE] = lax.rsqrt(degree)
-
-    pl.semaphore_wait(barrier, greeted)
+    for copy in column_copies:
+        copy.wait()
+    every_start = jnp.concatenate([columns[j][:col_width] for j in range(nx)], 0)
+    prev_ref[...] = every_start
+    cur_ref[...] = every_start
 
     def neighbour_copy(step, o):
         return pltpu.make_async_remote_copy(
@@ -97,10 +117,10 @@
         for t in range(tiles):
             at = slice(t * TILE, (t + 1) * TILE)
             scaled = (scale_ref[:, at] * cur_ref[:, at]).astype(jnp.bfloat16)
-            buf[t] = scaled.astype(jnp.float32)
+            buf[t] = scaled
         for o, d in enumerate(DISTANCES):
-            picked = jnp.concatenate([buf[send_ids[o, s]] for s in range(SLOTS)], 0)
-            outgoing[step, o] = picked.astype(jnp.bfloat16)
+            for s in range(SLOTS):
+                outgoing[step, o, s] = buf[send_ids[s, o]]
 
             @pl.when(jnp.logical_and(r + d >= 0, r + d < n))
             def _():
@@ -111,9 +131,7 @@
             @pl.when(jnp.logical_and(r - d >= 0, r - d < n))
             def _():
                 neighbour_copy(step, o).wait_recv()
-                arrived = incoming[step, o].astype(jnp.float32)
-                for s in range(SLOTS):
-                    buf[tiles + o * SLOTS + s] = arrived[s * SUB : (s + 1) * SUB]
+                buf[tiles + o * SLOTS : tiles + (o + 1) * SLOTS] = incoming[step, o]
 
         first = order == 0
         gain = jnp.where(first, 1.0 / filter_half, 2.0 / filter_half)
@@ -122,10 +140,10 @@
         for t in range(tiles):
             at = slice(t * TILE, (t + 1) * TILE)
             count = block_count[t]
-            blocks = [buf[jnp.where(b < count, col_ids[t, b], empty)] for b in range(NB)]
-            product = times_tile(t, jnp.concatenate(blocks, 1).astype(jnp.bfloat16))
+            blocks = [buf[jnp.where(b < count, col_ids[b, t], empty)] for b in range(NB)]
+            product = times_tile(t, jnp.concatenate(blocks, 1))
             current = cur_ref[:, at]
-            laplacian = current - scale_ref[:, at] * (product + buf[t])
+            laplacian = current - scale_ref[:, at] * (product + buf[t].astype(jnp.float32))
             following = gain * (laplacian - filter_center * current) - keep * prev_ref[:, at]
             prev_ref[:, at] = current
             cur_ref[:, at] = following
@@ -143,24 +161,14 @@
         return copies
 
     def orthonormalize(iteration):
-        columns[iteration, x] = cur_ref[...]
-        mine = columns.at[iteration, x]
-        pending = exchange([
-            pltpu.make_async_remote_copy(
-                src_ref=mine, dst_ref=mine,
-                send_sem=col_send.at[iteration, j], recv_sem=col_recv.at[iteration, j],
-                device_id=(r, (x + j) % nx), device_id_type=MESH,
-            )
-            for j in range(1, nx)
-        ])
-        every = jnp.concatenate([columns[iteration, j][:col_width] for j in range(nx)], 0)
+        every = cur_ref[...]
         partial = lax.dot_general(
             every, every, (((1,), (1,)), ((), ())),
             precision=lax.Precision.HIGHEST, preferred_element_type=jnp.float32,
         )
         gram_a[iteration, my_place, :, 0:K] = partial
         mine_a = gram_a.at[iteration, my_place]
-        pending += exchange([
+        pending = exchange([
             pltpu.make_async_remote_copy(
                 src_ref=mine_a, dst_ref=mine_a,
                 send_sem=a_send.at[iteration, j], recv_sem=a_recv.at[iteration, j],
@@ -189,7 +197,7 @@
         pivots = jnp.sum(jnp.where(row == lane, gram, 0.0), axis=1, keepdims=True)
         inverse = inverse * lax.rsqrt(pivots)
         combined = jnp.dot(
-            mixing_ref[iteration, x], inverse,
+            mixing_ref[iteration], inverse,
             precision=lax.Precision.HIGHEST, preferred_element_type=jnp.float32,
         )
         vectors = jnp.dot(
@@ -211,7 +219,11 @@
         return carry
 
     lax.fori_loop(0, ITERS, one_iteration, 0)
-    out_ref[...] = cur_ref[...]
+    for j in range(nx):
+
+        @pl.when(x == j)
+        def _():
+            out_ref[...] = cur_ref[j * col_width : (j + 1) * col_width]
 
 
 def body(start, weights, block_count, col_ids, send_ids, mixing):
@@ -220,45 +232,47 @@
     n, nx = lax.axis_size("rows"), lax.axis_size("cols")
     group = 4 if n % 4 == 0 else 1
     pad = SUB - col_width
-    mixing = mixing.reshape(ITERS, nx, col_width, K)
     if pad:
         start = jnp.pad(start, ((0, pad), (0, 0)))
-        mixing = jnp.pad(mixing, ((0, 0), (0, 0), (0, pad), (0, 0)))
     steps = ITERS * DEGREE
     vmem = pl.BlockSpec(memory_space=pltpu.VMEM)
-    smem = pl.BlockSpec(memory_space=pltpu.SMEM)
     dma = pltpu.SemaphoreType.DMA
     out = pl.pallas_call(
         functools.partial(kernel, n, nx, group, col_width, tiles, float(points * n)),
-        out_shape=jax.ShapeDtypeStruct((SUB, points), jnp.float32),
-        in_specs=[smem, smem, smem, vmem, vmem, pl.BlockSpec(memory_space=pl.ANY)],
+        out_shape=jax.ShapeDtypeStruct((col_width, points), jnp.float32),
+        in_specs=[pl.BlockSpec(memory_space=pl.ANY)] * 6,
         out_specs=vmem,
         scratch_shapes=[
+            pltpu.SMEM(block_count.shape, jnp.int32),
+            pltpu.SMEM(col_ids.shape[::-1], jnp.int32),
+            pltpu.SMEM(send_ids.shape[::-1], jnp.int32),
+            pltpu.VMEM(mixing.shape, jnp.float32),
             pltpu.VMEM(weights.shape, jnp.bfloat16),
-            pltpu.VMEM((SUB, points), jnp.float32),
-            pltpu.VMEM((SUB, points), jnp.float32),
-            pltpu.VMEM((SUB, points), jnp.float32),
-            pltpu.VMEM((tiles + 2 * REACH * SLOTS + 1, SUB, TILE), jnp.float32),
-            pltpu.VMEM((steps, 2 * REACH, SLOTS * SUB, TILE), jnp.bfloat16),
-            pltpu.VMEM((steps, 2 * REACH, SLOTS * SUB, TILE), jnp.bfloat16),
-            pltpu.VMEM((ITERS, nx, SUB, points), jnp.float32),
+            pltpu.VMEM((K, points), jnp.float32),
+            pltpu.VMEM((K, points), jnp.float32),
+            pltpu.VMEM((K, points), jnp.float32),
+            pltpu.VMEM((tiles + 2 * REACH * SLOTS + 1, K, TILE), jnp.bfloat16),
+            pltpu.VMEM((steps, 2 * REACH, SLOTS, K, TILE), jnp.bfloat16),
+            pltpu.VMEM((steps, 2 * REACH, SLOTS, K, TILE), jnp.bfloat16),
+            pltpu.VMEM((nx, SUB, points), jnp.float32),
             pltpu.VMEM((ITERS, group, K, TILE), jnp.float32),
             pltpu.VMEM((ITERS, n // group, K, TILE), jnp.float32),
             dma((tiles,)),
+            dma((5,)),
             dma((steps, 2 * REACH)),
             dma((steps, 2 * REACH)),
-            dma((ITERS, nx)),
-            dma((ITERS, nx)),
+            dma((nx,)),
+            dma((nx,)),
             dma((ITERS, group)),
             dma((ITERS, group)),
             dma((ITERS, n // group)),
             dma((ITERS, n // group)),
         ],
         compiler_params=pltpu.CompilerParams(
-            collective_id=0, has_side_effects=True, vmem_limit_bytes=32 * 1024 * 1024
+            collective_id=0, has_side_effects=True, vmem_limit_bytes=56 * 1024 * 1024
         ),
-    )(block_count, col_ids, send_ids, start, mixing, weights)
-    return out[:col_width]
+    )(block_count, col_ids.T, send_ids.T, start, mixing, weights)
+    return out
 
 
 def solution(mesh):

time: 72.8 us -> 63.6 us (0.87)
  local copies, waits for them, and re-layouts: 6.55 us -> 1.47 us
  Pallas kernels: 66 us -> 62 us
    unnamed x11 -> x1, local copies, waits for them, and re-layouts: 6.55 us -> 1.47 us
    pallas_call x1, Pallas kernels: 66 us -> 62 us  [body(): pl.pallas_call(functools.partial(kernel, n, nx, group, col_width, tiles,...]
where the time goes in v2:
time: 63.6 us; the launch traced here: 63.5 us
  Pallas kernels  62 us (97%)
  local copies, waits for them, and re-layouts  1.47 us (2%)
    pallas_call x1, Pallas kernels, body(): pl.pallas_call(functools.partial(kernel, n, nx, group, col_width, tiles,...  62 us
    unnamed x1, local copies, waits for them, and re-layouts  1.47 us

profile of v2, /device:TPU:0, one launch (start us, length us, event | category | flops | bytes accessed | tf_op | source)
XLA Modules:
  0.0 63.5 jit_solution(14887281424501479540)
XLA Ops:
  0.0 62.0 %shard_map.64 = f32[8,2048]{1,0:T(8,128)} custom-call(s32[16]{0:T(128)} %count_hbm.1, s32[8,16]{1,0:T(8,128)} %bitcast.2, s32[2,4]{1,0:T(2,128)} %bitcast.3, f32[8,2048]{1,0:T(8,128)} %start_hbm.1, f32[2,16,16]{2,1,0:T(8,128)} %mixing_hbm.1, bf16[16,8,128,128]{3,2,1,0:T(8,128)(2,1)} %weights_hbm.1), custom_call_target="tpu_custom_call" | custom-call | tf_op jit(solution)/shard_map/pallas_call | solution.py:240
  62.0 1.5 %copy.8 = f32[8,2048]{1,0:T(8,128)} copy(f32[8,2048]{1,0:T(8,128)} %shard_map.64) | data formatting | bytes 131072

commit v3 on v2

--- a/solution.py
+++ b/solution.py
@@ -48,6 +48,7 @@
         load.start()
     buf[tiles:] = jnp.zeros((buf.shape[0] - tiles, K, TILE), jnp.bfloat16)
     gram_a[...] = jnp.zeros_like(gram_a)
+    gram_b[...] = jnp.zeros_like(gram_b)
 
     barrier = pltpu.get_barrier_semaphore()
     greeted = (nx - 1) + (group - 1) + (n_groups - 1)
@@ -112,8 +113,7 @@
             device_id_type=MESH,
         )
 
-    def apply(iteration, order):
-        step = iteration * DEGREE + order
+    def apply(step, order):
         for t in range(tiles):
             at = slice(t * TILE, (t + 1) * TILE)
             scaled = (scale_ref[:, at] * cur_ref[:, at]).astype(jnp.bfloat16)
@@ -133,7 +133,7 @@
                 neighbour_copy(step, o).wait_recv()
                 buf[tiles + o * SLOTS : tiles + (o + 1) * SLOTS] = incoming[step, o]
 
-        first = order == 0
+        first = jnp.equal(order, 0)
         gain = jnp.where(first, 1.0 / filter_half, 2.0 / filter_half)
         keep = jnp.where(first, 0.0, 1.0)
         empty = tiles + 2 * REACH * SLOTS
@@ -153,42 +153,54 @@
             def _():
                 neighbour_copy(step, o).wait_send()
 
-    def exchange(copies):
-        for copy in copies:
-            copy.start()
-        for copy in copies:
-            copy.wait_recv()
-        return copies
-
-    def orthonormalize(iteration):
+    def group_copies(iteration):
+        mine = gram_a.at[iteration, my_place]
+        return [
+            pltpu.make_async_remote_copy(
+                src_ref=mine, dst_ref=mine,
+                send_sem=a_send.at[iteration, j], recv_sem=a_recv.at[iteration, j],
+                device_id=(my_group * group + (my_place + j) % group, x), device_id_type=MESH,
+            )
+            for j in range(1, group)
+        ]
+
+    def across_copies(iteration):
+        mine = gram_b.at[iteration, my_group]
+        return [
+            pltpu.make_async_remote_copy(
+                src_ref=mine, dst_ref=mine,
+                send_sem=b_send.at[iteration, j], recv_sem=b_recv.at[iteration, j],
+                device_id=((my_group + j) % n_groups * group + my_place, x), device_id_type=MESH,
+            )
+            for j in range(1, n_groups)
+        ]
+
+    def start_gram(iteration):
         every = cur_ref[...]
         partial = lax.dot_general(
             every, every, (((1,), (1,)), ((), ())),
             precision=lax.Precision.HIGHEST, preferred_element_type=jnp.float32,
         )
-        gram_a[iteration, my_place, :, 0:K] = partial
-        mine_a = gram_a.at[iteration, my_place]
-        pending = exchange([
-            pltpu.make_async_remote_copy(
-                src_ref=mine_a, dst_ref=mine_a,
-                send_sem=a_send.at[iteration, j], recv_sem=a_recv.at[iteration, j],
-                device_id=(my_group * group + (my_place + j) % group, x), device_id_type=MESH,
-            )
-            for j in range(1, group)
-        ])
+        gram_a[iteration, my_place, :, 0:K] = partial[:SUB]
+        gram_a[iteration, my_place, :, K : 2 * K] = partial[SUB:]
+        pending = group_copies(iteration)
+        for copy in pending:
+            copy.start()
+        for copy in pending:
+            copy.wait()
         gram_b[iteration, my_group] = sum(gram_a[iteration, j] for j in range(group))
-        mine_b = gram_b.at[iteration, my_group]
-        pending += exchange([
-            pltpu.make_async_remote_copy(
-                src_ref=mine_b, dst_ref=mine_b,
-                send_sem=b_send.at[iteration, j], recv_sem=b_recv.at[iteration, j],
-                device_id=((my_group + j) % n_groups * group + my_place, x), device_id_type=MESH,
-            )
-            for j in range(1, n_groups)
-        ])
-        gram = sum(gram_b[iteration, j] for j in range(n_groups)) / total_points
-        row = lax.broadcasted_iota(jnp.int32, (K, TILE), 0)
-        lane = lax.broadcasted_iota(jnp.int32, (K, TILE), 1)
+        pending = across_copies(iteration)
+        for copy in pending:
+            copy.start()
+        return pending
+
+    def finish_gram(iteration, pending):
+        for copy in pending:
+            copy.wait_recv()
+        packed = sum(gram_b[iteration, j] for j in range(n_groups)) / total_points
+        gram = jnp.concatenate([packed[:, :K], packed[:, K : 2 * K]], 0)
+        row = lax.broadcasted_iota(jnp.int32, (K, K), 0)
+        lane = lax.broadcasted_iota(jnp.int32, (K, K), 1)
         inverse = jnp.where(row == lane, 1.0, 0.0)
         for j in range(K - 1):
             factor = jnp.where(row > j, gram[:, j : j + 1] / gram[j : j + 1, j : j + 1], 0.0)
@@ -196,41 +208,47 @@
             gram = gram - factor * gram[j : j + 1]
         pivots = jnp.sum(jnp.where(row == lane, gram, 0.0), axis=1, keepdims=True)
         inverse = inverse * lax.rsqrt(pivots)
-        combined = jnp.dot(
+        return jnp.dot(
             mixing_ref[iteration], inverse,
             precision=lax.Precision.HIGHEST, preferred_element_type=jnp.float32,
         )
-        vectors = jnp.dot(
-            combined[:, :K], every,
+
+    def mixed(combined, vectors):
+        return jnp.dot(
+            combined, vectors,
             precision=lax.Precision.HIGHEST, preferred_element_type=jnp.float32,
         )
-        prev_ref[...] = vectors
-        cur_ref[...] = vectors
+
+    def one_step(step, carry):
+        apply(step, step % DEGREE)
+        return carry
+
+    lax.fori_loop(0, DEGREE, one_step, 0)
+    for iteration in range(ITERS):
+        pending = start_gram(iteration)
+        if iteration < ITERS - 1:
+            apply((iteration + 1) * DEGREE, 0)
+            combined = finish_gram(iteration, pending)
+            prev_ref[...] = mixed(combined, prev_ref[...])
+            cur_ref[...] = mixed(combined, cur_ref[...])
+            lax.fori_loop((iteration + 1) * DEGREE + 1, (iteration + 2) * DEGREE, one_step, 0)
+        else:
+            combined = finish_gram(iteration, pending)
+            for j in range(nx):
+
+                @pl.when(x == j)
+                def _():
+                    out_ref[...] = mixed(combined[j * col_width : (j + 1) * col_width], cur_ref[...])
+
         for copy in pending:
             copy.wait_send()
-
-    def one_iteration(iteration, carry):
-        def one_order(order, inner):
-            apply(iteration, order)
-            return inner
-
-        lax.fori_loop(0, DEGREE, one_order, 0)
-        orthonormalize(iteration)
-        return carry
-
-    lax.fori_loop(0, ITERS, one_iteration, 0)
-    for j in range(nx):
-
-        @pl.when(x == j)
-        def _():
-            out_ref[...] = cur_ref[j * col_width : (j + 1) * col_width]
 
 
 def body(start, weights, block_count, col_ids, send_ids, mixing):
     tiles = weights.shape[0]
     col_width, points = start.shape
     n, nx = lax.axis_size("rows"), lax.axis_size("cols")
-    group = 4 if n % 4 == 0 else 1
+    group = 4 if n > 16 and n % 4 == 0 else 1
     pad = SUB - col_width
     if pad:
         start = jnp.pad(start, ((0, pad), (0, 0)))
@@ -255,8 +273,8 @@
             pltpu.VMEM((steps, 2 * REACH, SLOTS, K, TILE), jnp.bfloat16),
             pltpu.VMEM((steps, 2 * REACH, SLOTS, K, TILE), jnp.bfloat16),
             pltpu.VMEM((nx, SUB, points), jnp.float32),
-            pltpu.VMEM((ITERS, group, K, TILE), jnp.float32),
-            pltpu.VMEM((ITERS, n // group, K, TILE), jnp.float32),
+            pltpu.VMEM((ITERS, group, SUB, TILE), jnp.float32),
+            pltpu.VMEM((ITERS, n // group, SUB, TILE), jnp.float32),
             dma((tiles,)),
             dma((5,)),
             dma((steps, 2 * REACH)),

time: 63.6 us -> 56.9 us (0.89)
  Pallas kernels: 62 us -> 55.2 us
    pallas_call x1, Pallas kernels: 62 us -> 55.2 us  [body(): pl.pallas_call(functools.partial(kernel, n, nx, group, col_width, tiles,...]
where the time goes in v3:
time: 56.9 us; the launch traced here: 56.7 us
  Pallas kernels  55.2 us (97%)
  local copies, waits for them, and re-layouts  1.47 us (3%)
    pallas_call x1, Pallas kernels, body(): pl.pallas_call(functools.partial(kernel, n, nx, group, col_width, tiles,...  55.2 us
    unnamed x1, local copies, waits for them, and re-layouts  1.47 us

profile of v3, /device:TPU:0, one launch (start us, length us, event | category | flops | bytes accessed | tf_op | source)
XLA Modules:
  0.0 56.7 jit_solution(10950058714505502045)
XLA Ops:
  0.0 55.2 %shard_map.64 = f32[8,2048]{1,0:T(8,128)} custom-call(s32[16]{0:T(128)} %count_hbm.1, s32[8,16]{1,0:T(8,128)} %bitcast.2, s32[2,4]{1,0:T(2,128)} %bitcast.3, f32[8,2048]{1,0:T(8,128)} %start_hbm.1, f32[2,16,16]{2,1,0:T(8,128)} %mixing_hbm.1, bf16[16,8,128,128]{3,2,1,0:T(8,128)(2,1)} %weights_hbm.1), custom_call_target="tpu_custom_call" | custom-call | tf_op jit(solution)/shard_map/pallas_call | solution.py:258
  55.2 1.5 %copy.8 = f32[8,2048]{1,0:T(8,128)} copy(f32[8,2048]{1,0:T(8,128)} %shard_map.64) | data formatting | bytes 131072

commit v4 on v3

--- a/solution.py
+++ b/solution.py
@@ -27,7 +27,7 @@
     n, nx, group, col_width, tiles, total_points,
     count_hbm, col_hbm, send_hbm, start_hbm, mixing_hbm, weights_hbm,
     out_ref,
-    block_count, col_ids, send_ids, mixing_ref,
+    block_count, col_ids, send_ids, sources, mixing_ref,
     w_ref, scale_ref, prev_ref, cur_ref, buf, outgoing, incoming, columns, gram_a, gram_b,
     w_sem, small_sem, send_sem, recv_sem, col_send, col_recv, a_send, a_recv, b_send, b_recv,
 ):
@@ -46,7 +46,7 @@
     loads = [pltpu.make_async_copy(weights_hbm.at[t], w_ref.at[t], w_sem.at[t]) for t in range(tiles)]
     for load in smalls + loads:
         load.start()
-    buf[tiles:] = jnp.zeros((buf.shape[0] - tiles, K, TILE), jnp.bfloat16)
+    buf[:, tiles:] = jnp.zeros((2, buf.shape[1] - tiles, K, TILE), jnp.bfloat16)
     gram_a[...] = jnp.zeros_like(gram_a)
     gram_b[...] = jnp.zeros_like(gram_b)
 
@@ -88,10 +88,13 @@
             blocks, w, (((1,), (1,)), ((), ())), preferred_element_type=jnp.float32
         )
 
+    empty = tiles + 2 * REACH * SLOTS
     for small in smalls:
         small.wait()
     for t in range(tiles):
         loads[t].wait()
+        for b in range(NB):
+            sources[b, t] = jnp.where(b < block_count[t], col_ids[b, t], empty)
         ones = [
             jnp.full((K, TILE), jnp.where(b < block_count[t], 1.0, 0.0), jnp.float32) for b in range(NB)
         ]
@@ -113,14 +116,17 @@
             device_id_type=MESH,
         )
 
-    def apply(step, order):
+    def rescale(slot):
         for t in range(tiles):
             at = slice(t * TILE, (t + 1) * TILE)
-            scaled = (scale_ref[:, at] * cur_ref[:, at]).astype(jnp.bfloat16)
-            buf[t] = scaled
+            buf[slot, t] = (scale_ref[:, at] * cur_ref[:, at]).astype(jnp.bfloat16)
+
+    def apply(step, order):
+        now = step % 2
+        later = 1 - now
         for o, d in enumerate(DISTANCES):
             for s in range(SLOTS):
-                outgoing[step, o, s] = buf[send_ids[s, o]]
+                outgoing[step, o, s] = buf[now, send_ids[s, o]]
 
             @pl.when(jnp.logical_and(r + d >= 0, r + d < n))
             def _():
@@ -131,27 +137,21 @@
             @pl.when(jnp.logical_and(r - d >= 0, r - d < n))
             def _():
                 neighbour_copy(step, o).wait_recv()
-                buf[tiles + o * SLOTS : tiles + (o + 1) * SLOTS] = incoming[step, o]
+                buf[now, tiles + o * SLOTS : tiles + (o + 1) * SLOTS] = incoming[step, o]
 
         first = jnp.equal(order, 0)
         gain = jnp.where(first, 1.0 / filter_half, 2.0 / filter_half)
         keep = jnp.where(first, 0.0, 1.0)
-        empty = tiles + 2 * REACH * SLOTS
         for t in range(tiles):
             at = slice(t * TILE, (t + 1) * TILE)
-            count = block_count[t]
-            blocks = [buf[jnp.where(b < count, col_ids[b, t], empty)] for b in range(NB)]
+            blocks = [buf[now, sources[b, t]] for b in range(NB)]
             product = times_tile(t, jnp.concatenate(blocks, 1))
             current = cur_ref[:, at]
-            laplacian = current - scale_ref[:, at] * (product + buf[t].astype(jnp.float32))
+            laplacian = current - scale_ref[:, at] * (product + buf[now, t].astype(jnp.float32))
             following = gain * (laplacian - filter_center * current) - keep * prev_ref[:, at]
             prev_ref[:, at] = current
             cur_ref[:, at] = following
-        for o, d in enumerate(DISTANCES):
-
-            @pl.when(jnp.logical_and(r + d >= 0, r + d < n))
-            def _():
-                neighbour_copy(step, o).wait_send()
+            buf[later, t] = (scale_ref[:, at] * following).astype(jnp.bfloat16)
 
     def group_copies(iteration):
         mine = gram_a.at[iteration, my_place]
@@ -223,6 +223,7 @@
         apply(step, step % DEGREE)
         return carry
 
+    rescale(0)
     lax.fori_loop(0, DEGREE, one_step, 0)
     for iteration in range(ITERS):
         pending = start_gram(iteration)
@@ -231,6 +232,7 @@
             combined = finish_gram(iteration, pending)
             prev_ref[...] = mixed(combined, prev_ref[...])
             cur_ref[...] = mixed(combined, cur_ref[...])
+            rescale(((iteration + 1) * DEGREE + 1) % 2)
             lax.fori_loop((iteration + 1) * DEGREE + 1, (iteration + 2) * DEGREE, one_step, 0)
         else:
             combined = finish_gram(iteration, pending)
@@ -242,6 +244,16 @@
 
         for copy in pending:
             copy.wait_send()
+
+    def one_sent(step, carry):
+        for o, d in enumerate(DISTANCES):
+
+            @pl.when(jnp.logical_and(r + d >= 0, r + d < n))
+            def _():
+                neighbour_copy(step, o).wait_send()
+        return carry
+
+    lax.fori_loop(0, ITERS * DEGREE, one_sent, 0)
 
 
 def body(start, weights, block_count, col_ids, send_ids, mixing):
@@ -264,12 +276,13 @@
             pltpu.SMEM(block_count.shape, jnp.int32),
             pltpu.SMEM(col_ids.shape[::-1], jnp.int32),
             pltpu.SMEM(send_ids.shape[::-1], jnp.int32),
+            pltpu.SMEM(col_ids.shape[::-1], jnp.int32),
             pltpu.VMEM(mixing.shape, jnp.float32),
             pltpu.VMEM(weights.shape, jnp.bfloat16),
             pltpu.VMEM((K, points), jnp.float32),
             pltpu.VMEM((K, points), jnp.float32),
             pltpu.VMEM((K, points), jnp.float32),
-            pltpu.VMEM((tiles + 2 * REACH * SLOTS + 1, K, TILE), jnp.bfloat16),
+            pltpu.VMEM((2, tiles + 2 * REACH * SLOTS + 1, K, TILE), jnp.bfloat16),
             pltpu.VMEM((steps, 2 * REACH, SLOTS, K, TILE), jnp.bfloat16),
             pltpu.VMEM((steps, 2 * REACH, SLOTS, K, TILE), jnp.bfloat16),
             pltpu.VMEM((nx, SUB, points), jnp.float32),

time: 56.9 us -> 76.3 us (1.34)
  Pallas kernels: 55.2 us -> 74.7 us
    pallas_call x1, Pallas kernels: 55.2 us -> 74.7 us  [body(): pl.pallas_call(functools.partial(kernel, n, nx, group, col_width, tiles,...]
where the time goes in v4:
time: 76.3 us; the launch traced here: 76.2 us
  Pallas kernels  74.7 us (98%)
  local copies, waits for them, and re-layouts  1.47 us (2%)
    pallas_call x1, Pallas kernels, body(): pl.pallas_call(functools.partial(kernel, n, nx, group, col_width, tiles,...  74.7 us

profile of v4, /device:TPU:0, one launch (start us, length us, event | category | flops | bytes accessed | tf_op | source)
XLA Modules:
  0.0 76.2 jit_solution(11698121117577932443)
XLA Ops:
  0.0 74.7 %shard_map.64 = f32[8,2048]{1,0:T(8,128)} custom-call(s32[16]{0:T(128)} %count_hbm.1, s32[8,16]{1,0:T(8,128)} %bitcast.2, s32[2,4]{1,0:T(2,128)} %bitcast.3, f32[8,2048]{1,0:T(8,128)} %start_hbm.1, f32[2,16,16]{2,1,0:T(8,128)} %mixing_hbm.1, bf16[16,8,128,128]{3,2,1,0:T(8,128)(2,1)} %weights_hbm.1), custom_call_target="tpu_custom_call" | custom-call | tf_op jit(solution)/shard_map/pallas_call | solution.py:270
  74.7 1.5 %copy.8 = f32[8,2048]{1,0:T(8,128)} copy(f32[8,2048]{1,0:T(8,128)} %shard_map.64) | data formatting | bytes 131072

commit v5 on v3

--- a/solution.py
+++ b/solution.py
@@ -27,7 +27,7 @@
     n, nx, group, col_width, tiles, total_points,
     count_hbm, col_hbm, send_hbm, start_hbm, mixing_hbm, weights_hbm,
     out_ref,
-    block_count, col_ids, send_ids, mixing_ref,
+    block_count, col_ids, send_ids, sources, mixing_ref,
     w_ref, scale_ref, prev_ref, cur_ref, buf, outgoing, incoming, columns, gram_a, gram_b,
     w_sem, small_sem, send_sem, recv_sem, col_send, col_recv, a_send, a_recv, b_send, b_recv,
 ):
@@ -88,10 +88,13 @@
             blocks, w, (((1,), (1,)), ((), ())), preferred_element_type=jnp.float32
         )
 
+    empty = tiles + 2 * REACH * SLOTS
     for small in smalls:
         small.wait()
     for t in range(tiles):
         loads[t].wait()
+        for b in range(NB):
+            sources[b, t] = jnp.where(b < block_count[t], col_ids[b, t], empty)
         ones = [
             jnp.full((K, TILE), jnp.where(b < block_count[t], 1.0, 0.0), jnp.float32) for b in range(NB)
         ]
@@ -136,22 +139,15 @@
         first = jnp.equal(order, 0)
         gain = jnp.where(first, 1.0 / filter_half, 2.0 / filter_half)
         keep = jnp.where(first, 0.0, 1.0)
-        empty = tiles + 2 * REACH * SLOTS
         for t in range(tiles):
             at = slice(t * TILE, (t + 1) * TILE)
-            count = block_count[t]
-            blocks = [buf[jnp.where(b < count, col_ids[b, t], empty)] for b in range(NB)]
+            blocks = [buf[sources[b, t]] for b in range(NB)]
             product = times_tile(t, jnp.concatenate(blocks, 1))
             current = cur_ref[:, at]
             laplacian = current - scale_ref[:, at] * (product + buf[t].astype(jnp.float32))
             following = gain * (laplacian - filter_center * current) - keep * prev_ref[:, at]
             prev_ref[:, at] = current
             cur_ref[:, at] = following
-        for o, d in enumerate(DISTANCES):
-
-            @pl.when(jnp.logical_and(r + d >= 0, r + d < n))
-            def _():
-                neighbour_copy(step, o).wait_send()
 
     def group_copies(iteration):
         mine = gram_a.at[iteration, my_place]
@@ -242,6 +238,16 @@
 
         for copy in pending:
             copy.wait_send()
+
+    def one_sent(step, carry):
+        for o, d in enumerate(DISTANCES):
+
+            @pl.when(jnp.logical_and(r + d >= 0, r + d < n))
+            def _():
+                neighbour_copy(step, o).wait_send()
+        return carry
+
+    lax.fori_loop(0, ITERS * DEGREE, one_sent, 0)
 
 
 def body(start, weights, block_count, col_ids, send_ids, mixing):
@@ -264,6 +270,7 @@
             pltpu.SMEM(block_count.shape, jnp.int32),
             pltpu.SMEM(col_ids.shape[::-1], jnp.int32),
             pltpu.SMEM(send_ids.shape[::-1], jnp.int32),
+            pltpu.SMEM(col_ids.shape[::-1], jnp.int32),
             pltpu.VMEM(mixing.shape, jnp.float32),
             pltpu.VMEM(weights.shape, jnp.bfloat16),
             pltpu.VMEM((K, points), jnp.float32),

time: 56.9 us -> 56.8 us (level)
  no operation moved by 1% of the time
where the time goes in v5:
time: 56.8 us; the launch traced here: 56.7 us
  Pallas kernels  55.2 us (97%)
  local copies, waits for them, and re-layouts  1.47 us (3%)
    pallas_call x1, Pallas kernels, body(): pl.pallas_call(functools.partial(kernel, n, nx, group, col_width, tiles,...  55.2 us
    unnamed x1, local copies, waits for them, and re-layouts  1.47 us

profile of v5, /device:TPU:0, one launch (start us, length us, event | category | flops | bytes accessed | tf_op | source)
XLA Modules:
  0.0 56.7 jit_solution(4957008334479797218)
XLA Ops:
  0.0 55.2 %shard_map.64 = f32[8,2048]{1,0:T(8,128)} custom-call(s32[16]{0:T(128)} %count_hbm.1, s32[8,16]{1,0:T(8,128)} %bitcast.2, s32[2,4]{1,0:T(2,128)} %bitcast.3, f32[8,2048]{1,0:T(8,128)} %start_hbm.1, f32[2,16,16]{2,1,0:T(8,128)} %mixing_hbm.1, bf16[16,8,128,128]{3,2,1,0:T(8,128)(2,1)} %weights_hbm.1), custom_call_target="tpu_custom_call" | custom-call | tf_op jit(solution)/shard_map/pallas_call | solution.py:264
  55.2 1.5 %copy.8 = f32[8,2048]{1,0:T(8,128)} copy(f32[8,2048]{1,0:T(8,128)} %shard_map.64) | data formatting | bytes 131072
